TPU v7x, 32 devices: a whole 2x2x4 slice. The times are simulated.
32 devices in a mesh: frame: 4 (over z), dom: 2 (over x), coef: 4 (over y, core).
Axes of the slice: x: 2, y: 2, z: 4, core: 2. Of those that a mesh axis runs over, the one named last changes fastest.
Arguments:
- geometry: float32 [32, 32768], P('coef', ('frame', 'dom')), may hold values from -1 to 1
- fraction: float32 [32, 32768], P('coef', ('frame', 'dom')), may hold values from 0 to 1
- interval: int32 [32, 32768], P('coef', ('frame', 'dom')), may hold values from 0 to 156
- pattern: int32 [32, 256], P('coef', ('frame', 'dom')), may hold values from 0 to 95
- target: float32 [32768], P(('frame', 'dom')), may hold values from -8 to 8
Outputs:
- solution: float32 [384, 160], P('coef')
- residual: float32 [32768], P(('frame', 'dom'))
Inputs may be any that keep to these rules, and one draw needn't show every extreme that they name: The spline of a slot reads coefficients interval to interval + 3 of its type. Slot s refers to pair type (s // 8) * 96 + pattern.
All inputs are finite; a program needn't handle non-finite values.
Results may differ from a plain program's by a relative error of at most 0.0003.
Values sent between devices are 32-bit elements; how exact they have to be, the bound alone decides.
A program may use at most 64 MiB of HBM per device.

v0:
```python
import math

import jax
import jax.numpy as jnp
from jax import lax
from jax.sharding import PartitionSpec as P

NK = 160
TYPES = 384
ITERS = 2


def spline_weights(fraction):
    square = fraction * fraction
    cube = square * fraction
    return (
        (1.0 - fraction) ** 3 / 6.0,
        (3.0 * cube - 6.0 * square + 4.0) / 6.0,
        (-3.0 * cube + 3.0 * square + 3.0 * fraction + 1.0) / 6.0,
        cube / 6.0,
    )


def dense_tiles(geom, fraction, interval):
    knots = lax.broadcasted_iota(jnp.int32, (1, NK, 1), 1)
    tiles = jnp.zeros((geom.shape[0], NK, geom.shape[1]), jnp.float32)
    for offset, weight in enumerate(spline_weights(fraction)):
        hit = knots == (interval + offset)[:, None, :]
        tiles = tiles + jnp.where(hit, (geom * weight)[:, None, :], 0.0)
    return tiles


def block_layout(geom):
    tiles_all = geom.shape[1] // 128
    block = math.gcd(8, tiles_all)
    return (block, block * 128, tiles_all // block)


def block_tiles(geometry, fraction, interval, pattern, index, block, width):
    start = index * width
    geom = lax.dynamic_slice_in_dim(geometry, start, width, 1)
    frac = lax.dynamic_slice_in_dim(fraction, start, width, 1)
    knot = lax.dynamic_slice_in_dim(interval, start, width, 1)
    kinds = lax.dynamic_slice_in_dim(pattern, index * block, block, 1)
    tiles = dense_tiles(geom, frac, knot).reshape(geom.shape[0], NK, block, 128)
    return (tiles, kinds, start)


def forward(coeffs, geometry, fraction, interval, pattern):
    block, width, count = block_layout(geometry)

    def forward_step(index, image):
        tiles, kinds, start = block_tiles(
            geometry, fraction, interval, pattern, index, block, width
        )
        chosen = jnp.take(coeffs, kinds, axis=0)
        part = jnp.einsum("sktr,stk->tr", tiles, chosen, precision=lax.Precision.HIGHEST)
        return lax.dynamic_update_slice_in_dim(image, part.reshape(width), start, 0)

    return lax.fori_loop(0, count, forward_step, jnp.zeros((geometry.shape[1],), jnp.float32))


def backward(resid, per_coef, geometry, fraction, interval, pattern):
    block, width, count = block_layout(geometry)
    owners = lax.broadcasted_iota(jnp.int32, (1, 1, per_coef), 2)

    def backward_step(index, total):
        tiles, kinds, start = block_tiles(
            geometry, fraction, interval, pattern, index, block, width
        )
        piece = lax.dynamic_slice_in_dim(resid, start, width, 0).reshape(block, 128)
        contrib = jnp.einsum("sktr,tr->stk", tiles, piece, precision=lax.Precision.HIGHEST)
        picks = (kinds[:, :, None] == owners).astype(jnp.float32)
        return total + jnp.einsum("stc,stk->ck", picks, contrib, precision=lax.Precision.HIGHEST)

    return lax.fori_loop(0, count, backward_step, jnp.zeros((per_coef, NK), jnp.float32))


def on_device(geometry, fraction, interval, pattern, target):
    per_coef = TYPES // lax.axis_size("coef")

    def transpose_sum(resid):
        local = backward(resid, per_coef, geometry, fraction, interval, pattern).reshape(
            per_coef * NK
        )
        share = lax.psum(local, ("frame", "dom"))
        total = lax.psum(jnp.sum(share * share), "coef")
        return (share, total)

    def expand(share):
        return share.reshape(per_coef, NK)

    residual = target
    gradient, gamma = transpose_sum(residual)
    direction = gradient
    solution = jnp.zeros_like(gradient)
    for step_index in range(ITERS):
        partial_image = forward(expand(direction), geometry, fraction, interval, pattern)
        image = lax.psum(partial_image, "coef")
        image_total = lax.psum(jnp.sum(image * image), ("frame", "dom"))
        alpha = gamma / image_total
        solution = solution + alpha * direction
        residual = residual - alpha * image
        if step_index + 1 < ITERS:
            gradient, gamma_next = transpose_sum(residual)
            direction = gradient + gamma_next / gamma * direction
            gamma = gamma_next
    return (expand(solution), residual)


def solution(mesh):
    in_specs = (
        P("coef", ("frame", "dom")),
        P("coef", ("frame", "dom")),
        P("coef", ("frame", "dom")),
        P("coef", ("frame", "dom")),
        P(("frame", "dom")),
    )
    out_specs = (P("coef", None), P(("frame", "dom")))
    return jax.shard_map(
        on_device, mesh=mesh, in_specs=in_specs, out_specs=out_specs, check_vma=False
    )
```

profile of v0, /device:TPU:0, one launch (start us, length us, event | category | flops | bytes accessed | tf_op | source)
XLA Modules:
  0.0 356.5 jit_solution(18207071083211695407)
XLA Ops:
  0.6 52.4 %while.56 = (s32[]{:T(128)}, f32[96,160]{0,1:T(8,128)S(1)}, s32[8,32]{1,0:T(8,128)}, f32[4096]{0:T(1024)}, s32[8,4096]{1,0:T(8,128)}, /*index=5*/f32[8,4096]{1,0...) while((s32[]{:T(128)}, f32[96,160]{0,1:T(8,128)S(1)}, ...), condition=%wide.region_1.2_spmd.clone, body=%wide.region_0.1_spmd.clone.sunk | while | flops 42192900 | bytes 11854863 | solution.py:76
  0.7 0.8 fusion.117
  2.4 1.9 select_add_fusion.10
  5.0 8.4 %fusion.118 = f32[8,1,8,160]{3,1,2,0:T(1,128)S(1)} fusion(f32[8,128,1,1]{1,2,3,0:T(1,128)S(1)} %bitcast.184, f32[8,160,8,128]{3,2,1,0:T(8,128)S(1)} %select_add_fusion.10), kind=kOutput, calls=%fused_computation.4.clone.1 | convolution fusion | flops 15728640 | bytes 5287936 | tf_op jit(solution)/shard_map/while/body/eval_jaxpr/sktr,tr->stk/dot_general | solution.py:72
  13.8 0.8 fusion.117
  15.5 1.9 select_add_fusion.10
  18.1 8.4 %fusion.118 = f32[8,1,8,160]{3,1,2,0:T(1,128)S(1)} fusion(f32[8,128,1,1]{1,2,3,0:T(1,128)S(1)} %bitcast.184, f32[8,160,8,128]{3,2,1,0:T(8,128)S(1)} %select_add_fusion.10), kind=kOutput, calls=%fused_computation.4.clone.1 | convolution fusion | flops 15728640 | bytes 5287936 | tf_op jit(solution)/shard_map/while/body/eval_jaxpr/sktr,tr->stk/dot_general | solution.py:72
  26.9 0.8 fusion.117
  28.6 1.9 select_add_fusion.10
  31.2 8.4 %fusion.118 = f32[8,1,8,160]{3,1,2,0:T(1,128)S(1)} fusion(f32[8,128,1,1]{1,2,3,0:T(1,128)S(1)} %bitcast.184, f32[8,160,8,128]{3,2,1,0:T(8,128)S(1)} %select_add_fusion.10), kind=kOutput, calls=%fused_computation.4.clone.1 | convolution fusion | flops 15728640 | bytes 5287936 | tf_op jit(solution)/shard_map/while/body/eval_jaxpr/sktr,tr->stk/dot_general | solution.py:72
  41.7 1.9 select_add_fusion.10
  44.3 8.4 %fusion.118 = f32[8,1,8,160]{3,1,2,0:T(1,128)S(1)} fusion(f32[8,128,1,1]{1,2,3,0:T(1,128)S(1)} %bitcast.184, f32[8,160,8,128]{3,2,1,0:T(8,128)S(1)} %select_add_fusion.10), kind=kOutput, calls=%fused_computation.4.clone.1 | convolution fusion | flops 15728640 | bytes 5287936 | tf_op jit(solution)/shard_map/while/body/eval_jaxpr/sktr,tr->stk/dot_general | solution.py:72
  53.3 39.3 %psum.56 = f32[15360]{0:T(1024)S(1)} all-reduce(f32[15360]{0:T(1024)S(1)} %reshape.226), channel_id=1, replica_groups=mesh['frame'=4,'dom'=2,'coef'=4] {'frame','dom'}, use_global_device_ids=true, to_apply=%region_2.3 | all-reduce | flops 15360 | bytes 122880 | tf_op jit(solution)/shard_map/psum | solution.py:86
  92.7 53.3 %while.54 = (s32[]{:T(128)}, f32[4096]{0:T(1024)S(1)}, s32[8,4096]{1,0:T(8,128)}, f32[8,4096]{1,0:T(8,128)}, f32[8,4096]{1,0:T(8,128)}, /*index=5*/s32[8,32]{1,0...) while((s32[]{:T(128)}, f32[4096]{0:T(1024)S(1)}, ...), condition=%wide.region_6.0_spmd, body=%wide.region_5.7_spmd.sunk | while | flops 30371208 | bytes 11859845 | solution.py:60
  94.5 4.2 %select_add_fusion.8 = f32[8,160,8,128]{3,2,1,0:T(8,128)} fusion(f32[8,8,128]{2,1,0:T(8,128)S(1)} %copy.152, s32[8,8,128]{2,1,0:T(8,128)S(1)} %copy.153, f32[8,8,128]{2,1,0:T(8,128)S(1)} %copy.154, s32[8,8,128]{2,1,0:T(8,128)S(1)} %copy.155, f32[8,8,128]{2,1,0:T(8,128)S(1)} %copy.156, s32[8,8,128]{2,1,0:T(8,128)S(1)} %copy.157, ...), kind=kLoop, calls=%fused_computation.82.clone.1 | loop fusion | flops 14417920 | bytes 5505024 | tf_op jit(solution)/shard_map/while/body/eval_jaxpr/add | solution.py:29
  99.6 6.1 %fusion.108 = f32[8,1,128,1]{2,1,3,0:T(1,128)S(1)} fusion(f32[8,160,8,128]{3,2,1,0:T(8,128)} %select_add_fusion.8, f32[8,8,160,1]{2,1,0,3:T(8,128)S(1)} %fusion.107), kind=kOutput, calls=%fused_computation.80.clone.1 | convolution fusion | flops 15728640 | bytes 5287936 | tf_op jit(solution)/shard_map/while/body/eval_jaxpr/sktr,stk->tr/dot_general | solution.py:57
  107.8 4.2 %select_add_fusion.8 = f32[8,160,8,128]{3,2,1,0:T(8,128)} fusion(f32[8,8,128]{2,1,0:T(8,128)S(1)} %copy.152, s32[8,8,128]{2,1,0:T(8,128)S(1)} %copy.153, f32[8,8,128]{2,1,0:T(8,128)S(1)} %copy.154, s32[8,8,128]{2,1,0:T(8,128)S(1)} %copy.155, f32[8,8,128]{2,1,0:T(8,128)S(1)} %copy.156, s32[8,8,128]{2,1,0:T(8,128)S(1)} %copy.157, ...), kind=kLoop, calls=%fused_computation.82.clone.1 | loop fusion | flops 14417920 | bytes 5505024 | tf_op jit(solution)/shard_map/while/body/eval_jaxpr/add | solution.py:29
  112.9 6.1 %fusion.108 = f32[8,1,128,1]{2,1,3,0:T(1,128)S(1)} fusion(f32[8,160,8,128]{3,2,1,0:T(8,128)} %select_add_fusion.8, f32[8,8,160,1]{2,1,0,3:T(8,128)S(1)} %fusion.107), kind=kOutput, calls=%fused_computation.80.clone.1 | convolution fusion | flops 15728640 | bytes 5287936 | tf_op jit(solution)/shard_map/while/body/eval_jaxpr/sktr,stk->tr/dot_general | solution.py:57
  119.4 0.8 fusion.106
  121.1 4.2 %select_add_fusion.8 = f32[8,160,8,128]{3,2,1,0:T(8,128)} fusion(f32[8,8,128]{2,1,0:T(8,128)S(1)} %copy.152, s32[8,8,128]{2,1,0:T(8,128)S(1)} %copy.153, f32[8,8,128]{2,1,0:T(8,128)S(1)} %copy.154, s32[8,8,128]{2,1,0:T(8,128)S(1)} %copy.155, f32[8,8,128]{2,1,0:T(8,128)S(1)} %copy.156, s32[8,8,128]{2,1,0:T(8,128)S(1)} %copy.157, ...), kind=kLoop, calls=%fused_computation.82.clone.1 | loop fusion | flops 14417920 | bytes 5505024 | tf_op jit(solution)/shard_map/while/body/eval_jaxpr/add | solution.py:29
  126.3 6.1 %fusion.108 = f32[8,1,128,1]{2,1,3,0:T(1,128)S(1)} fusion(f32[8,160,8,128]{3,2,1,0:T(8,128)} %select_add_fusion.8, f32[8,8,160,1]{2,1,0,3:T(8,128)S(1)} %fusion.107), kind=kOutput, calls=%fused_computation.80.clone.1 | convolution fusion | flops 15728640 | bytes 5287936 | tf_op jit(solution)/shard_map/while/body/eval_jaxpr/sktr,stk->tr/dot_general | solution.py:57
  134.4 4.2 %select_add_fusion.8 = f32[8,160,8,128]{3,2,1,0:T(8,128)} fusion(f32[8,8,128]{2,1,0:T(8,128)S(1)} %copy.152, s32[8,8,128]{2,1,0:T(8,128)S(1)} %copy.153, f32[8,8,128]{2,1,0:T(8,128)S(1)} %copy.154, s32[8,8,128]{2,1,0:T(8,128)S(1)} %copy.155, f32[8,8,128]{2,1,0:T(8,128)S(1)} %copy.156, s32[8,8,128]{2,1,0:T(8,128)S(1)} %copy.157, ...), kind=kLoop, calls=%fused_computation.82.clone.1 | loop fusion | flops 14417920 | bytes 5505024 | tf_op jit(solution)/shard_map/while/body/eval_jaxpr/add | solution.py:29
  139.6 6.1 %fusion.108 = f32[8,1,128,1]{2,1,3,0:T(1,128)S(1)} fusion(f32[8,160,8,128]{3,2,1,0:T(8,128)} %select_add_fusion.8, f32[8,8,160,1]{2,1,0,3:T(8,128)S(1)} %fusion.107), kind=kOutput, calls=%fused_computation.80.clone.1 | convolution fusion | flops 15728640 | bytes 5287936 | tf_op jit(solution)/shard_map/while/body/eval_jaxpr/sktr,stk->tr/dot_general | solution.py:57
  146.6 11.3 %all-reduce = (f32[4096]{0:T(1024)S(1)}, f32[]{:T(128)}) all-reduce(f32[4096]{0:T(1024)S(1)} %get-tuple-element.530, f32[]{:T(128)} %multiply_reduce_fusion.1), channel_id=1, replica_groups=mesh['frame'=4,'dom'=2,'coef'=4] {'coef'}, use_global_device_ids=true, to_apply=%region_7.9 | all-reduce | flops 4097 | bytes 32776 | tf_op jit(solution)/shard_map/psum | solution.py:99
  158.5 18.0 %psum.59 = f32[]{:T(128)} all-reduce(f32[]{:T(128)} %multiply_reduce_fusion.3), channel_id=1, replica_groups=mesh['frame'=4,'dom'=2,'coef'=4] {'frame','dom'}, use_global_device_ids=true, to_apply=%region_9.11 | all-reduce | flops 1 | bytes 8 | tf_op jit(solution)/shard_map/psum | solution.py:100
  177.8 49.7 %while.57 = (s32[]{:T(128)}, f32[96,160]{0,1:T(8,128)S(1)}, s32[8,32]{1,0:T(8,128)}, f32[4096]{0:T(1024)S(1)}, s32[8,4096]{1,0:T(8,128)}, /*index=5*/f32[8,4096]...) while((s32[]{:T(128)}, f32[96,160]{0,1:T(8,128)S(1)}, ...), condition=%wide.region_11.13_spmd.clone, body=%wide.region_10.12_spmd.clone.sunk | while | flops 42192900 | bytes 11854863 | solution.py:76
  179.6 1.9 select_add_fusion.11
  181.5 8.4 %fusion.124 = f32[8,1,8,160]{3,1,2,0:T(1,128)S(1)} fusion(f32[8,128,1,1]{1,2,3,0:T(1,128)S(1)} %bitcast.185, f32[8,160,8,128]{3,2,1,0:T(8,128)S(1)} %select_add_fusion.11), kind=kOutput, calls=%fused_computation.42.clone.1 | convolution fusion | flops 15728640 | bytes 5287936 | tf_op jit(solution)/shard_map/while/body/eval_jaxpr/sktr,tr->stk/dot_general | solution.py:72
  192.0 1.9 select_add_fusion.11
  193.9 8.4 %fusion.124 = f32[8,1,8,160]{3,1,2,0:T(1,128)S(1)} fusion(f32[8,128,1,1]{1,2,3,0:T(1,128)S(1)} %bitcast.185, f32[8,160,8,128]{3,2,1,0:T(8,128)S(1)} %select_add_fusion.11), kind=kOutput, calls=%fused_computation.42.clone.1 | convolution fusion | flops 15728640 | bytes 5287936 | tf_op jit(solution)/shard_map/while/body/eval_jaxpr/sktr,tr->stk/dot_general | solution.py:72
  204.4 1.9 select_add_fusion.11
  206.4 8.4 %fusion.124 = f32[8,1,8,160]{3,1,2,0:T(1,128)S(1)} fusion(f32[8,128,1,1]{1,2,3,0:T(1,128)S(1)} %bitcast.185, f32[8,160,8,128]{3,2,1,0:T(8,128)S(1)} %select_add_fusion.11), kind=kOutput, calls=%fused_computation.42.clone.1 | convolution fusion | flops 15728640 | bytes 5287936 | tf_op jit(solution)/shard_map/while/body/eval_jaxpr/sktr,tr->stk/dot_general | solution.py:72
  216.9 1.9 select_add_fusion.11
  218.8 8.4 %fusion.124 = f32[8,1,8,160]{3,1,2,0:T(1,128)S(1)} fusion(f32[8,128,1,1]{1,2,3,0:T(1,128)S(1)} %bitcast.185, f32[8,160,8,128]{3,2,1,0:T(8,128)S(1)} %select_add_fusion.11), kind=kOutput, calls=%fused_computation.42.clone.1 | convolution fusion | flops 15728640 | bytes 5287936 | tf_op jit(solution)/shard_map/while/body/eval_jaxpr/sktr,tr->stk/dot_general | solution.py:72
  227.8 35.4 %psum.60 = f32[15360]{0:T(1024)S(1)} all-reduce(f32[15360]{0:T(1024)S(1)} %reshape.228), channel_id=1, replica_groups=mesh['frame'=4,'dom'=2,'coef'=4] {'frame','dom'}, use_global_device_ids=true, to_apply=%region_12.14 | all-reduce | flops 15360 | bytes 122880 | tf_op jit(solution)/shard_map/psum | solution.py:86
  263.8 6.7 %psum.61 = f32[]{:T(128)} all-reduce(f32[]{:T(128)} %multiply_reduce_fusion), channel_id=1, replica_groups=mesh['frame'=4,'dom'=2,'coef'=4] {'coef'}, use_global_device_ids=true, to_apply=%region_14.16 | all-reduce | flops 1 | bytes 8 | tf_op jit(solution)/shard_map/psum | solution.py:87
  272.0 53.3 %while.55 = (s32[]{:T(128)}, f32[4096]{0:T(1024)S(1)}, s32[8,4096]{1,0:T(8,128)}, f32[8,4096]{1,0:T(8,128)}, f32[8,4096]{1,0:T(8,128)}, /*index=5*/s32[8,32]{1,0...) while((s32[]{:T(128)}, f32[4096]{0:T(1024)S(1)}, ...), condition=%wide.region_16.18_spmd, body=%wide.region_15.17_spmd.sunk | while | flops 30371208 | bytes 11859845 | solution.py:60
  273.7 4.2 %select_add_fusion.9 = f32[8,160,8,128]{3,2,1,0:T(8,128)} fusion(f32[8,8,128]{2,1,0:T(8,128)S(1)} %copy.162, s32[8,8,128]{2,1,0:T(8,128)S(1)} %copy.163, f32[8,8,128]{2,1,0:T(8,128)S(1)} %copy.164, s32[8,8,128]{2,1,0:T(8,128)S(1)} %copy.165, f32[8,8,128]{2,1,0:T(8,128)S(1)} %copy.166, s32[8,8,128]{2,1,0:T(8,128)S(1)} %copy.167, ...), kind=kLoop, calls=%fused_computation.119.clone.1 | loop fusion | flops 14417920 | bytes 5505024 | tf_op jit(solution)/shard_map/while/body/eval_jaxpr/add | solution.py:29
  278.9 6.1 %fusion.113 = f32[8,1,128,1]{2,1,3,0:T(1,128)S(1)} fusion(f32[8,160,8,128]{3,2,1,0:T(8,128)} %select_add_fusion.9, f32[8,8,160,1]{2,1,0,3:T(8,128)S(1)} %fusion.112), kind=kOutput, calls=%fused_computation.117.clone.1 | convolution fusion | flops 15728640 | bytes 5287936 | tf_op jit(solution)/shard_map/while/body/eval_jaxpr/sktr,stk->tr/dot_general | solution.py:57
  287.1 4.2 %select_add_fusion.9 = f32[8,160,8,128]{3,2,1,0:T(8,128)} fusion(f32[8,8,128]{2,1,0:T(8,128)S(1)} %copy.162, s32[8,8,128]{2,1,0:T(8,128)S(1)} %copy.163, f32[8,8,128]{2,1,0:T(8,128)S(1)} %copy.164, s32[8,8,128]{2,1,0:T(8,128)S(1)} %copy.165, f32[8,8,128]{2,1,0:T(8,128)S(1)} %copy.166, s32[8,8,128]{2,1,0:T(8,128)S(1)} %copy.167, ...), kind=kLoop, calls=%fused_computation.119.clone.1 | loop fusion | flops 14417920 | bytes 5505024 | tf_op jit(solution)/shard_map/while/body/eval_jaxpr/add | solution.py:29
  292.2 6.1 %fusion.113 = f32[8,1,128,1]{2,1,3,0:T(1,128)S(1)} fusion(f32[8,160,8,128]{3,2,1,0:T(8,128)} %select_add_fusion.9, f32[8,8,160,1]{2,1,0,3:T(8,128)S(1)} %fusion.112), kind=kOutput, calls=%fused_computation.117.clone.1 | convolution fusion | flops 15728640 | bytes 5287936 | tf_op jit(solution)/shard_map/while/body/eval_jaxpr/sktr,stk->tr/dot_general | solution.py:57
  300.4 4.2 %select_add_fusion.9 = f32[8,160,8,128]{3,2,1,0:T(8,128)} fusion(f32[8,8,128]{2,1,0:T(8,128)S(1)} %copy.162, s32[8,8,128]{2,1,0:T(8,128)S(1)} %copy.163, f32[8,8,128]{2,1,0:T(8,128)S(1)} %copy.164, s32[8,8,128]{2,1,0:T(8,128)S(1)} %copy.165, f32[8,8,128]{2,1,0:T(8,128)S(1)} %copy.166, s32[8,8,128]{2,1,0:T(8,128)S(1)} %copy.167, ...), kind=kLoop, calls=%fused_computation.119.clone.1 | loop fusion | flops 14417920 | bytes 5505024 | tf_op jit(solution)/shard_map/while/body/eval_jaxpr/add | solution.py:29
  305.5 6.1 %fusion.113 = f32[8,1,128,1]{2,1,3,0:T(1,128)S(1)} fusion(f32[8,160,8,128]{3,2,1,0:T(8,128)} %select_add_fusion.9, f32[8,8,160,1]{2,1,0,3:T(8,128)S(1)} %fusion.112), kind=kOutput, calls=%fused_computation.117.clone.1 | convolution fusion | flops 15728640 | bytes 5287936 | tf_op jit(solution)/shard_map/while/body/eval_jaxpr/sktr,stk->tr/dot_general | solution.py:57
  312.0 0.8 fusion.111
  313.7 4.2 %select_add_fusion.9 = f32[8,160,8,128]{3,2,1,0:T(8,128)} fusion(f32[8,8,128]{2,1,0:T(8,128)S(1)} %copy.162, s32[8,8,128]{2,1,0:T(8,128)S(1)} %copy.163, f32[8,8,128]{2,1,0:T(8,128)S(1)} %copy.164, s32[8,8,128]{2,1,0:T(8,128)S(1)} %copy.165, f32[8,8,128]{2,1,0:T(8,128)S(1)} %copy.166, s32[8,8,128]{2,1,0:T(8,128)S(1)} %copy.167, ...), kind=kLoop, calls=%fused_computation.119.clone.1 | loop fusion | flops 14417920 | bytes 5505024 | tf_op jit(solution)/shard_map/while/body/eval_jaxpr/add | solution.py:29
  318.8 6.1 %fusion.113 = f32[8,1,128,1]{2,1,3,0:T(1,128)S(1)} fusion(f32[8,160,8,128]{3,2,1,0:T(8,128)} %select_add_fusion.9, f32[8,8,160,1]{2,1,0,3:T(8,128)S(1)} %fusion.112), kind=kOutput, calls=%fused_computation.117.clone.1 | convolution fusion | flops 15728640 | bytes 5287936 | tf_op jit(solution)/shard_map/while/body/eval_jaxpr/sktr,stk->tr/dot_general | solution.py:57
  325.3 10.1 %psum.62 = f32[4096]{0:T(1024)S(1)} all-reduce(f32[4096]{0:T(1024)S(1)} %get-tuple-element.532), channel_id=1, replica_groups=mesh['frame'=4,'dom'=2,'coef'=4] {'coef'}, use_global_device_ids=true, to_apply=%region_17.19 | all-reduce | flops 4096 | bytes 32768 | tf_op jit(solution)/shard_map/psum | solution.py:99
  336.0 17.8 %psum.63 = f32[]{:T(128)} all-reduce(f32[]{:T(128)} %multiply_reduce_fusion.2), channel_id=1, replica_groups=mesh['frame'=4,'dom'=2,'coef'=4] {'frame','dom'}, use_global_device_ids=true, to_apply=%region_19.21 | all-reduce | flops 1 | bytes 8 | tf_op jit(solution)/shard_map/psum | solution.py:100
  (281 shorter events, 42.3 us)
Async XLA Ops:
  4.3 9.1 %copy-start = (s32[8,32]{1,0:T(8,128)S(1)}, s32[8,32]{1,0:T(8,128)}, u32[]{:S(2)}) copy-start(s32[8,32]{1,0:T(8,128)} %get-tuple-element.953) | copy-start | bytes 3076 | tf_op jit(solution)/shard_map/while
  17.4 9.1 %copy-start = (s32[8,32]{1,0:T(8,128)S(1)}, s32[8,32]{1,0:T(8,128)}, u32[]{:S(2)}) copy-start(s32[8,32]{1,0:T(8,128)} %get-tuple-element.953) | copy-start | bytes 3076 | tf_op jit(solution)/shard_map/while
  30.5 9.1 %copy-start = (s32[8,32]{1,0:T(8,128)S(1)}, s32[8,32]{1,0:T(8,128)}, u32[]{:S(2)}) copy-start(s32[8,32]{1,0:T(8,128)} %get-tuple-element.953) | copy-start | bytes 3076 | tf_op jit(solution)/shard_map/while
  43.6 9.1 %copy-start = (s32[8,32]{1,0:T(8,128)S(1)}, s32[8,32]{1,0:T(8,128)}, u32[]{:S(2)}) copy-start(s32[8,32]{1,0:T(8,128)} %get-tuple-element.953) | copy-start | bytes 3076 | tf_op jit(solution)/shard_map/while
  92.7 85.1 %copy-start.4 = (f32[4096]{0:T(1024)S(1)}, f32[4096]{0:T(1024)}, u32[]{:S(2)}) copy-start(f32[4096]{0:T(1024)} %get-tuple-element.1094) | copy-start | bytes 49156
  92.7 6.0 %copy-start.1 = (s32[8,32]{1,0:T(8,128)S(1)}, s32[8,32]{1,0:T(8,128)}, u32[]{:S(2)}) copy-start(s32[8,32]{1,0:T(8,128)} %get-tuple-element.995) | copy-start | bytes 3076 | tf_op jit(solution)/shard_map/while
  106.1 6.0 %copy-start.1 = (s32[8,32]{1,0:T(8,128)S(1)}, s32[8,32]{1,0:T(8,128)}, u32[]{:S(2)}) copy-start(s32[8,32]{1,0:T(8,128)} %get-tuple-element.995) | copy-start | bytes 3076 | tf_op jit(solution)/shard_map/while
  119.4 6.0 %copy-start.1 = (s32[8,32]{1,0:T(8,128)S(1)}, s32[8,32]{1,0:T(8,128)}, u32[]{:S(2)}) copy-start(s32[8,32]{1,0:T(8,128)} %get-tuple-element.995) | copy-start | bytes 3076 | tf_op jit(solution)/shard_map/while
  132.7 6.0 %copy-start.1 = (s32[8,32]{1,0:T(8,128)S(1)}, s32[8,32]{1,0:T(8,128)}, u32[]{:S(2)}) copy-start(s32[8,32]{1,0:T(8,128)} %get-tuple-element.995) | copy-start | bytes 3076 | tf_op jit(solution)/shard_map/while
  181.5 8.4 %copy-start.2 = (s32[8,32]{1,0:T(8,128)S(1)}, s32[8,32]{1,0:T(8,128)}, u32[]{:S(2)}) copy-start(s32[8,32]{1,0:T(8,128)} %get-tuple-element.1031) | copy-start | bytes 3076 | tf_op jit(solution)/shard_map/while
  193.9 8.4 %copy-start.2 = (s32[8,32]{1,0:T(8,128)S(1)}, s32[8,32]{1,0:T(8,128)}, u32[]{:S(2)}) copy-start(s32[8,32]{1,0:T(8,128)} %get-tuple-element.1031) | copy-start | bytes 3076 | tf_op jit(solution)/shard_map/while
  206.3 8.4 %copy-start.2 = (s32[8,32]{1,0:T(8,128)S(1)}, s32[8,32]{1,0:T(8,128)}, u32[]{:S(2)}) copy-start(s32[8,32]{1,0:T(8,128)} %get-tuple-element.1031) | copy-start | bytes 3076 | tf_op jit(solution)/shard_map/while
  218.8 8.4 %copy-start.2 = (s32[8,32]{1,0:T(8,128)S(1)}, s32[8,32]{1,0:T(8,128)}, u32[]{:S(2)}) copy-start(s32[8,32]{1,0:T(8,128)} %get-tuple-element.1031) | copy-start | bytes 3076 | tf_op jit(solution)/shard_map/while
  272.0 6.0 %copy-start.3 = (s32[8,32]{1,0:T(8,128)S(1)}, s32[8,32]{1,0:T(8,128)}, u32[]{:S(2)}) copy-start(s32[8,32]{1,0:T(8,128)} %get-tuple-element.1073) | copy-start | bytes 3076 | tf_op jit(solution)/shard_map/while
  285.3 6.0 %copy-start.3 = (s32[8,32]{1,0:T(8,128)S(1)}, s32[8,32]{1,0:T(8,128)}, u32[]{:S(2)}) copy-start(s32[8,32]{1,0:T(8,128)} %get-tuple-element.1073) | copy-start | bytes 3076 | tf_op jit(solution)/shard_map/while
  298.6 6.0 %copy-start.3 = (s32[8,32]{1,0:T(8,128)S(1)}, s32[8,32]{1,0:T(8,128)}, u32[]{:S(2)}) copy-start(s32[8,32]{1,0:T(8,128)} %get-tuple-element.1073) | copy-start | bytes 3076 | tf_op jit(solution)/shard_map/while
  312.0 6.0 %copy-start.3 = (s32[8,32]{1,0:T(8,128)S(1)}, s32[8,32]{1,0:T(8,128)}, u32[]{:S(2)}) copy-start(s32[8,32]{1,0:T(8,128)} %get-tuple-element.1073) | copy-start | bytes 3076 | tf_op jit(solution)/shard_map/while
where the time goes:
time: 359 us; the launch traced here: 357 us
  blocking collectives  139 us (39%)
  matrix products  118 us (33%)
  other arithmetic  78.9 us (22%)
  local copies, waits for them, and re-layouts  14.3 us (4%)
  between operations  4.8 us (1%)
    psum x2, blocking collectives, transpose_sum(): share = lax.psum(local, ('frame', 'dom'))  74.7 us
    dot_general x8, matrix products, backward_step(): jnp.einsum('sktr,tr->stk', tiles, piece, precision=lax.Precision.HIGHEST)  66.9 us
    add x16, other arithmetic, dense_tiles(): tiles = tiles + jnp.where(hit, (geom * weight)[:, None, :], 0.0)  49.2 us
    dot_general x8, matrix products, forward_step(): jnp.einsum('sktr,stk->tr', tiles, chosen, precision=lax.Precision.HIGHEST)  49 us
    psum x2, blocking collectives, on_device(): image_total = lax.psum(jnp.sum(image * image), ('frame', 'dom'))  35.7 us
    psum x2, blocking collectives, on_device(): image = lax.psum(partial_image, 'coef')  21.4 us
    broadcast_in_dim x16, other arithmetic, dense_tiles(): tiles = tiles + jnp.where(hit, (geom * weight)[:, None, :], 0.0)  13 us
    while x16, other arithmetic  12.4 us

commit v1 on v0

v1 whole, which is shorter than its diff:
```python
import functools

import jax
import jax.numpy as jnp
from jax import lax
from jax.experimental import pallas as pl
from jax.experimental.pallas import tpu as pltpu
from jax.sharding import PartitionSpec as P

NK = 160
TYPES = 384
LANES = 128
LOW = 16
HIGHS = NK // LOW
SPREAD = LOW + 4
MESH = pl.DeviceIdType.MESH
F32 = jnp.float32
BF16 = jnp.bfloat16


def iota(shape, axis):
    return lax.broadcasted_iota(jnp.int32, shape, axis)


def split(x):
    top = x.astype(BF16)
    return top, (x - top.astype(F32)).astype(BF16)


def total_of(x):
    return jnp.sum(jnp.sum(x, axis=0, keepdims=True), axis=1, keepdims=True)


def each(count, body):
    if count <= 8:
        for index in range(count):
            body(index)
    else:
        lax.fori_loop(0, count, lambda index, _: (body(index), 0)[1], 0)


def kernel(n, nd, nc, share, geom_ref, frac_ref, knot_ref, patt_ref, targ_ref, sol_ref, res_ref,
           gw, z, table, picks, picks_t, fold, send_buf, rs_buf, ag_buf, im_buf, fin_buf,
           rs_send, rs_recv, ag_send, ag_recv, im_send, im_recv, fin_send, fin_recv):
    nb, rows = geom_ref.shape
    tiles = rows // LANES
    pairs = tiles * nb
    per_coef = TYPES // nc
    wide = picks.shape[1] // 2
    quarter = per_coef // 4
    at_dom = lax.axis_index("dom")
    at_coef = lax.axis_index("coef")
    at_frame = lax.axis_index("frame")
    me = at_frame * nd + at_dom

    def member(step):
        return lax.rem(me + step, n)

    def member_id(p):
        return (lax.div(p, nd), lax.rem(p, nd), at_coef)

    def coef_peer(step):
        return lax.rem(at_coef + step, nc)

    def coef_id(p):
        return (at_frame, at_dom, p)

    barrier = pltpu.get_barrier_semaphore()
    each(n - 1, lambda k: pl.semaphore_signal(barrier, inc=1, device_id=member_id(member(k + 1)), device_id_type=MESH))
    each(nc - 1, lambda k: pl.semaphore_signal(barrier, inc=1, device_id=coef_id(coef_peer(k + 1)), device_id_type=MESH))

    kinds = patt_ref[...].astype(F32).astype(BF16)
    spread = (iota((tiles, pairs), 1) >= nb * iota((tiles, pairs), 0)) & (iota((tiles, pairs), 1) < nb * (iota((tiles, pairs), 0) + 1))
    across = jnp.dot(kinds, jnp.where(spread, 1.0, 0.0).astype(BF16), preferred_element_type=F32)
    own = (iota((nb, pairs), 1) & (nb - 1)) == iota((nb, pairs), 0)
    across = jnp.sum(jnp.where(own, across, 0.0), axis=0, keepdims=True).astype(jnp.int32)
    hot_t = jnp.where(across == iota((per_coef, pairs), 0), 1.0, 0.0).astype(BF16)
    picks_t[...] = jnp.concatenate([hot_t, hot_t], axis=1)
    spread = (iota((pairs, tiles), 0) >= nb * iota((pairs, tiles), 1)) & (iota((pairs, tiles), 0) < nb * (iota((pairs, tiles), 1) + 1))
    down = lax.dot_general(jnp.where(spread, 1.0, 0.0).astype(BF16), kinds, (((1,), (1,)), ((), ())), preferred_element_type=F32)
    own = (iota((pairs, nb), 0) & (nb - 1)) == iota((pairs, nb), 1)
    down = jnp.sum(jnp.where(own, down, 0.0), axis=1, keepdims=True).astype(jnp.int32)
    hot = jnp.where(down == iota((pairs, wide), 1), 1.0, 0.0).astype(BF16)
    picks[...] = jnp.concatenate([hot, hot], axis=1)
    lows = iota((SPREAD * nb, 2 * LANES), 0) // nb
    for h in range(HIGHS):
        fold[h] = jnp.where(iota((SPREAD * nb, 2 * LANES), 1) == lows + LOW * h, 1.0, 0.0).astype(BF16)

    same_slot = (iota((HIGHS * nb, SPREAD * nb), 0) & (nb - 1)) == (iota((HIGHS * nb, SPREAD * nb), 1) & (nb - 1))

    def weigh(at):
        u = frac_ref[:, at]
        g = geom_ref[:, at] * (1.0 / 6.0)
        square = u * u
        cube = square * u
        less = 1.0 - u
        gw[0, :, at] = g * (less * less * less)
        gw[1, :, at] = g * (3.0 * cube - 6.0 * square + 4.0)
        gw[2, :, at] = g * (-3.0 * cube + 3.0 * square + 3.0 * u + 1.0)
        gw[3, :, at] = g * cube

    def backward(value_ref, first):
        def block(b, carry):
            values = value_ref[pl.ds(pl.multiple_of(8 * b, 8), 8), :]
            for k in range(8):
                at = pl.ds(pl.multiple_of((8 * b + k) * LANES, LANES), LANES)
                if first:
                    weigh(at)
                knot = knot_ref[:, at]
                high, low = knot >> 4, knot & (LOW - 1)
                value = values[k:k + 1, :]
                terms = [gw[j, :, at] * value for j in range(4)]
                hits = [low == m for m in range(LOW)]
                parts = []
                for m in range(SPREAD):
                    part = jnp.zeros((nb, LANES), F32)
                    for j in range(4):
                        if 0 <= m - j < LOW:
                            part = jnp.where(hits[m - j], terms[j], part)
                    parts.append(part)
                right = jnp.concatenate(split(jnp.concatenate(parts, axis=0)), axis=1)
                left = jnp.concatenate([jnp.where(high == h, 1.0, 0.0) for h in range(HIGHS)], axis=0).astype(BF16)
                left = jnp.concatenate([left, left], axis=1)
                prod = lax.dot_general(left, right, (((1,), (1,)), ((), ())), preferred_element_type=F32)
                prod = jnp.where(same_slot, prod, 0.0)
                for h in range(HIGHS):
                    z[h, pl.ds(pl.multiple_of((8 * b + k) * nb, nb), nb), :] = prod[h * nb:(h + 1) * nb, :]
            return carry

        lax.fori_loop(0, tiles // 8, block, 0)
        grad = jnp.zeros((per_coef, 2 * LANES), F32)
        for h in range(HIGHS):
            chosen = jnp.dot(picks_t[...], jnp.concatenate(split(z[h]), axis=0), preferred_element_type=F32)
            for piece in split(chosen):
                grad = grad + jnp.dot(piece, fold[h], preferred_element_type=F32)
        tail = grad[:quarter, LANES:]
        for q in range(1, 4):
            tail = tail + pltpu.roll(grad[q * quarter:(q + 1) * quarter, LANES:], 32 * q, 1)
        filled = per_coef + quarter
        return jnp.concatenate([grad[:, :LANES], tail, jnp.zeros((n * share - filled, LANES), F32)], axis=0)

    def tails(packed):
        tail = packed[per_coef:per_coef + quarter, :]
        return [tail] + [pltpu.roll(tail, LANES - 32 * q, 1) for q in range(1, 4)]

    def forward(packed, out):
        upper = jnp.concatenate(tails(packed) + [jnp.zeros((wide - per_coef, LANES), F32)], axis=0)
        lower = jnp.concatenate([packed[:per_coef, :], jnp.zeros((wide - per_coef, LANES), F32)], axis=0)
        coeffs = jnp.concatenate([lower, upper], axis=1)
        table[...] = jnp.dot(picks[...], jnp.concatenate(split(coeffs), axis=0), preferred_element_type=F32)

        def block(b, carry):
            sums = []
            for k in range(8):
                at = pl.ds(pl.multiple_of((8 * b + k) * LANES, LANES), LANES)
                span = pl.ds(pl.multiple_of((8 * b + k) * nb, nb), nb)
                below, above = table[span, :LANES], table[span, LANES:]
                knot = knot_ref[:, at]
                force = jnp.zeros((nb, LANES), F32)
                for j in range(4):
                    index = knot + j
                    lane = index & (LANES - 1)
                    found = jnp.where(
                        index < LANES,
                        jnp.take_along_axis(below, lane, axis=1, mode="promise_in_bounds"),
                        jnp.take_along_axis(above, lane, axis=1, mode="promise_in_bounds"),
                    )
                    force = force + gw[j, :, at] * found
                sums.append(jnp.sum(force, axis=0, keepdims=True))
            im_buf[out, at_coef, pl.ds(pl.multiple_of(8 * b, 8), 8), :] = jnp.concatenate(sums, axis=0)
            return carry

        lax.fori_loop(0, tiles // 8, block, 0)
        im_buf[out, at_coef, tiles:tiles + 8, :] = jnp.broadcast_to(total_of(packed * packed), (8, LANES))

    def copies(kind, phase, step):
        p = member(step) if kind != "im" else coef_peer(step)
        if kind == "rs":
            count = share + 8 * phase
            return (send_buf.at[phase, p, pl.ds(0, count)], rs_buf.at[phase, me, pl.ds(0, count)], rs_send.at[phase, p], rs_recv.at[phase, me], member_id(p))
        if kind == "ag":
            return (ag_buf.at[phase, me], ag_buf.at[phase, me], ag_send.at[phase, p], ag_recv.at[phase, me], member_id(p))
        if kind == "im":
            return (im_buf.at[phase, at_coef], im_buf.at[phase, at_coef], im_send.at[phase, p], im_recv.at[phase, at_coef], coef_id(p))
        return (fin_buf.at[me], fin_buf.at[me], fin_send.at[p], fin_recv.at[me], member_id(p))

    def landing(kind, phase, step):
        p = member(step) if kind != "im" else coef_peer(step)
        if kind == "rs":
            count = share + 8 * phase
            return (send_buf.at[phase, p, pl.ds(0, count)], rs_buf.at[phase, p, pl.ds(0, count)], rs_send.at[phase, p], rs_recv.at[phase, p], member_id(p))
        if kind == "ag":
            return (ag_buf.at[phase, p], ag_buf.at[phase, p], ag_send.at[phase, p], ag_recv.at[phase, p], member_id(p))
        if kind == "im":
            return (im_buf.at[phase, p], im_buf.at[phase, p], im_send.at[phase, p], im_recv.at[phase, p], coef_id(p))
        return (fin_buf.at[p], fin_buf.at[p], fin_send.at[p], fin_recv.at[p], member_id(p))

    def remote(parts):
        return pltpu.make_async_remote_copy(src_ref=parts[0], dst_ref=parts[1], send_sem=parts[2], recv_sem=parts[3], device_id=parts[4], device_id_type=MESH)

    def start(kind, phase, count):
        each(count - 1, lambda k: remote(copies(kind, phase, k + 1)).start())

    def arrive(kind, phase, count):
        each(count - 1, lambda k: remote(landing(kind, phase, k + 1)).wait_recv())

    def drain(kind, phase, count):
        each(count - 1, lambda k: remote(copies(kind, phase, k + 1)).wait_send())

    def scatter_sum(packed, phase, extra):
        for p in range(n):
            send_buf[phase, p, :share, :] = packed[p * share:(p + 1) * share, :]
            if extra is not None:
                send_buf[phase, p, share:share + 8, :] = jnp.broadcast_to(extra, (8, LANES))
        start("rs", phase, n)
        rs_buf[phase, me] = send_buf[phase, me]
        arrive("rs", phase, n)
        sums = rs_buf[phase, 0]
        for p in range(1, n):
            sums = sums + rs_buf[phase, p]
        return sums

    def gather(part, phase):
        ag_buf[phase, me] = part
        start("ag", phase, n)
        arrive("ag", phase, n)
        return ag_buf[phase].reshape(n * share, LANES)

    def exchange(phase):
        start("im", phase, nc)
        arrive("im", phase, nc)
        sums = im_buf[phase, 0]
        for p in range(1, nc):
            sums = sums + im_buf[phase, p]
        return sums[:tiles], sums[tiles:tiles + 1, :1]

    packed = backward(targ_ref, True)
    send_buf[...] = jnp.zeros(send_buf.shape, F32)
    pl.semaphore_wait(barrier, n - 1 + nc - 1)
    part = scatter_sum(packed, 0, None)[:share]
    grad = gather(part, 0)
    forward(grad, 0)
    image, gamma = exchange(0)
    res_ref[...] = image
    packed = backward(res_ref, False)
    sums = scatter_sum(packed, 1, total_of(image * image))
    alpha = gamma / sums[share:share + 1, :1]
    part = part - alpha * sums[:share]
    grad_next = gather(part, 1)
    forward(grad_next, 1)
    image_next, gamma_next = exchange(1)
    beta = gamma_next / gamma
    image_next = image_next + beta * image
    fin_buf[me] = jnp.broadcast_to(total_of(image_next * image_next), (8, LANES))
    start("fin", 0, n)
    direction = grad_next + beta * grad
    arrive("fin", 0, n)
    norm = fin_buf[0, :1, :1]
    for p in range(1, n):
        norm = norm + fin_buf[p, :1, :1]
    alpha_next = gamma_next / norm
    answer = alpha * grad + alpha_next * direction
    sol_ref[:, :LANES] = answer[:per_coef]
    for q, tail in enumerate(tails(answer)):
        sol_ref[q * quarter:(q + 1) * quarter, LANES:] = tail[:, :NK - LANES]
    res_ref[...] = targ_ref[...] - alpha * image - alpha_next * image_next
    for phase in range(2):
        drain("rs", phase, n)
        drain("ag", phase, n)
        drain("im", phase, nc)
    drain("fin", 0, n)


def on_device(n, nd, nc, geometry, fraction, interval, pattern, target):
    nb, rows = geometry.shape
    tiles = rows // LANES
    pairs = tiles * nb
    per_coef = TYPES // nc
    wide = -(-per_coef // LANES) * LANES
    share = -(-(per_coef + per_coef // 4) // (8 * n)) * 8
    sem = pltpu.SemaphoreType.DMA
    vmem = pl.BlockSpec(memory_space=pltpu.VMEM)
    solved, left = pl.pallas_call(
        functools.partial(kernel, n, nd, nc, share),
        out_shape=(jax.ShapeDtypeStruct((per_coef, NK), F32), jax.ShapeDtypeStruct((tiles, LANES), F32)),
        in_specs=[vmem] * 5,
        out_specs=(vmem, vmem),
        scratch_shapes=[
            pltpu.VMEM((4, nb, rows), F32),
            pltpu.VMEM((HIGHS, pairs, SPREAD * nb), F32),
            pltpu.VMEM((pairs, 2 * LANES), F32),
            pltpu.VMEM((pairs, 2 * wide), BF16),
            pltpu.VMEM((per_coef, 2 * pairs), BF16),
            pltpu.VMEM((HIGHS, SPREAD * nb, 2 * LANES), BF16),
            pltpu.VMEM((2, n, share + 8, LANES), F32),
            pltpu.VMEM((2, n, share + 8, LANES), F32),
            pltpu.VMEM((2, n, share, LANES), F32),
            pltpu.VMEM((2, nc, tiles + 8, LANES), F32),
            pltpu.VMEM((n, 8, LANES), F32),
            sem((2, n)), sem((2, n)), sem((2, n)), sem((2, n)), sem((2, nc)), sem((2, nc)), sem((n,)), sem((n,)),
        ],
        compiler_params=pltpu.CompilerParams(collective_id=0, has_side_effects=True, vmem_limit_bytes=40 * 1024 * 1024),
    )(geometry, fraction, interval, pattern, target.reshape(tiles, LANES))
    return solved, left.reshape(rows)


def solution(mesh):
    sizes = dict(mesh.shape)
    n, nd, nc = sizes["frame"] * sizes["dom"], sizes["dom"], sizes["coef"]
    both = P("coef", ("frame", "dom"))
    return jax.shard_map(
        functools.partial(on_device, n, nd, nc),
        mesh=mesh,
        in_specs=(both, both, both, both, P(("frame", "dom"))),
        out_specs=(P("coef", None), P(("frame", "dom"))),
        check_vma=False,
    )
```

time: 359 us -> 45.9 us (0.13)
  blocking collectives: 139 us -> 0 us
  matrix products: 118 us -> 0 us
  other arithmetic: 78.9 us -> 0 us
  Pallas kernels: 0 us -> 39.5 us
  local copies, waits for them, and re-layouts: 14.3 us -> 5.45 us
  between operations: 4.8 us -> 0.65 us
    psum x7 -> x0, blocking collectives: 139 us -> none  [the longest x2 74.7 us: transpose_sum(): share = lax.psum(local, ('frame', 'dom'))]
    dot_general x24 -> x0, matrix products: 118 us -> none  [the longest x8 66.9 us: backward_step(): jnp.einsum('sktr,tr->stk', tiles, piece, precision=lax.Precision.HIGHEST)]
    add x18 -> x0, other arithmetic: 49.2 us -> none  [the longest x16 49.2 us: dense_tiles(): tiles = tiles + jnp.where(hit, (geom * weight)[:, None, :], 0.0)]
    pallas_call x0 -> x1, Pallas kernels: none -> 39.5 us  [on_device(): pl.pallas_call(functools.partial(kernel, n, nd, nc, share), out_shape=(ja...]
    broadcast_in_dim x16 -> x0, other arithmetic: 13 us -> none  [dense_tiles(): tiles = tiles + jnp.where(hit, (geom * weight)[:, None, :], 0.0)]
    while x16 -> x0, other arithmetic: 12.4 us -> none
    gather x8 -> x0, local copies, waits for them, and re-layouts: 5.25 us -> none  [forward_step(): chosen = jnp.take(coeffs, kinds, axis=0)]
    unnamed x3 -> x12, local copies, waits for them, and re-layouts: 0.74 us -> 5.45 us
where the time goes in v1:
time: 45.9 us; the launch traced here: 45.6 us
  Pallas kernels  39.5 us (86%)
  local copies, waits for them, and re-layouts  5.45 us (12%)
  between operations  0.65 us (1%)
    pallas_call x1, Pallas kernels, on_device(): pl.pallas_call(functools.partial(kernel, n, nd, nc, share), out_shape=(ja...  39.5 us
    unnamed x12, local copies, waits for them, and re-layouts  5.45 us

profile of v1, /device:TPU:0, one launch (start us, length us, event | category | flops | bytes accessed | tf_op | source)
XLA Modules:
  0.0 45.6 jit_solution(12390929724142359489)
XLA Ops:
  0.6 0.0 copy-start
  0.6 0.9 %copy-done = f32[8,4096]{1,0:T(8,128)S(1)} copy-done((f32[8,4096]{1,0:T(8,128)S(1)}, f32[8,4096]{1,0:T(8,128)}, u32[]{:S(2)}) %copy-start) | copy-done | bytes 131096
  1.5 0.0 copy-start.1
  1.5 0.9 %copy-done.1 = f32[8,4096]{1,0:T(8,128)S(1)} copy-done((f32[8,4096]{1,0:T(8,128)S(1)}, f32[8,4096]{1,0:T(8,128)}, u32[]{:S(2)}) %copy-start.1) | copy-done | bytes 131096
  2.4 0.0 copy-start.2
  2.4 0.9 %copy-done.2 = s32[8,4096]{1,0:T(8,128)S(1)} copy-done((s32[8,4096]{1,0:T(8,128)S(1)}, s32[8,4096]{1,0:T(8,128)}, u32[]{:S(2)}) %copy-start.2) | copy-done | bytes 131096
  3.3 0.0 copy-start.3
  3.3 0.7 %copy-done.3 = f32[4096]{0:T(1024)S(1)} copy-done((f32[4096]{0:T(1024)S(1)}, f32[4096]{0:T(1024)}, u32[]{:S(2)}) %copy-start.3) | copy-done | bytes 16408
  4.1 0.0 copy-start.4
  4.1 0.7 %copy-done.4 = s32[8,32]{1,0:T(8,128)S(1)} copy-done((s32[8,32]{1,0:T(8,128)S(1)}, s32[8,32]{1,0:T(8,128)}, u32[]{:S(2)}) %copy-start.4) | copy-done | bytes 1048
  4.8 39.5 %shard_map.68 = (f32[96,160]{1,0:T(8,128)S(1)}, f32[32,128]{1,0:T(8,128)S(1)}) custom-call(f32[8,4096]{1,0:T(8,128)S(1)} %copy-done, f32[8,4096]{1,0:T(8,128)S(1)} %copy-done.1, s32[8,4096]{1,0:T(8,128)S(1)} %copy-done.2, s32[8,32]{1,0:T(8,128)S(1)} %copy-done.4, f32[32,128]{1,0:T(8,128)S(1)} %bitcast.2), custom_call_target="tpu_custom_call" | custom-call | tf_op jit(solution)/shard_map/pallas_call | solution.py:283
  44.3 0.7 %copy.7 = f32[96,160]{0,1:T(8,128)} copy(f32[96,160]{1,0:T(8,128)S(1)} %get-tuple-element.6) | data formatting | bytes 122880
  45.0 0.6 %copy.9 = f32[4096]{0:T(1024)} copy(f32[4096]{0:T(1024)S(1)} %bitcast.3) | data formatting | bytes 32768
Async XLA Ops:
  0.6 0.9 %copy-start = (f32[8,4096]{1,0:T(8,128)S(1)}, f32[8,4096]{1,0:T(8,128)}, u32[]{:S(2)}) copy-start(f32[8,4096]{1,0:T(8,128)} %geom_ref.1) | copy-start | bytes 393220
  1.5 0.9 %copy-start.1 = (f32[8,4096]{1,0:T(8,128)S(1)}, f32[8,4096]{1,0:T(8,128)}, u32[]{:S(2)}) copy-start(f32[8,4096]{1,0:T(8,128)} %frac_ref.1) | copy-start | bytes 393220
  2.4 0.9 %copy-start.2 = (s32[8,4096]{1,0:T(8,128)S(1)}, s32[8,4096]{1,0:T(8,128)}, u32[]{:S(2)}) copy-start(s32[8,4096]{1,0:T(8,128)} %knot_ref.1) | copy-start | bytes 393220
  3.3 0.7 %copy-start.3 = (f32[4096]{0:T(1024)S(1)}, f32[4096]{0:T(1024)}, u32[]{:S(2)}) copy-start(f32[4096]{0:T(1024)} %param.9) | copy-start | bytes 49156
  4.1 0.7 %copy-start.4 = (s32[8,32]{1,0:T(8,128)S(1)}, s32[8,32]{1,0:T(8,128)}, u32[]{:S(2)}) copy-start(s32[8,32]{1,0:T(8,128)} %patt_ref.1) | copy-start | bytes 3076

commit v2 on v1

--- a/solution.py
+++ b/solution.py
@@ -39,9 +39,16 @@
         lax.fori_loop(0, count, lambda index, _: (body(index), 0)[1], 0)
 
 
-def kernel(n, nd, nc, share, geom_ref, frac_ref, knot_ref, patt_ref, targ_ref, sol_ref, res_ref,
-           gw, z, table, picks, picks_t, fold, send_buf, rs_buf, ag_buf, im_buf, fin_buf,
-           rs_send, rs_recv, ag_send, ag_recv, im_send, im_recv, fin_send, fin_recv):
+def kernel(n, nd, nc, share, geom_hbm, frac_hbm, knot_hbm, patt_hbm, targ_hbm, sol_ref, res_ref,
+           geom_ref, frac_ref, knot_ref, patt_ref, targ_ref, image_ref,
+           gw, z, table, picks, picks_t, fold, send_buf, rs_buf, ag_buf, im_buf, gm_buf, nm_buf, load_sem,
+           rs_send, rs_recv, ag_send, ag_recv, im_send, im_recv, gm_send, gm_recv, nm_send, nm_recv):
+    loads = [
+        pltpu.make_async_copy(src, dst, load_sem.at[k])
+        for k, (src, dst) in enumerate(((patt_hbm, patt_ref), (frac_hbm, frac_ref), (geom_hbm, geom_ref), (knot_hbm, knot_ref), (targ_hbm, targ_ref)))
+    ]
+    for load in loads:
+        load.start()
     nb, rows = geom_ref.shape
     tiles = rows // LANES
     pairs = tiles * nb
@@ -69,6 +76,12 @@
     each(n - 1, lambda k: pl.semaphore_signal(barrier, inc=1, device_id=member_id(member(k + 1)), device_id_type=MESH))
     each(nc - 1, lambda k: pl.semaphore_signal(barrier, inc=1, device_id=coef_id(coef_peer(k + 1)), device_id_type=MESH))
 
+    lows = iota((SPREAD * nb, 2 * LANES), 0) // nb
+    for h in range(HIGHS):
+        fold[h] = jnp.where(iota((SPREAD * nb, 2 * LANES), 1) == lows + LOW * h, 1.0, 0.0).astype(BF16)
+    same_slot = (iota((HIGHS * nb, SPREAD * nb), 0) & (nb - 1)) == (iota((HIGHS * nb, SPREAD * nb), 1) & (nb - 1))
+
+    loads[0].wait()
     kinds = patt_ref[...].astype(F32).astype(BF16)
     spread = (iota((tiles, pairs), 1) >= nb * iota((tiles, pairs), 0)) & (iota((tiles, pairs), 1) < nb * (iota((tiles, pairs), 0) + 1))
     across = jnp.dot(kinds, jnp.where(spread, 1.0, 0.0).astype(BF16), preferred_element_type=F32)
@@ -82,11 +95,8 @@
     down = jnp.sum(jnp.where(own, down, 0.0), axis=1, keepdims=True).astype(jnp.int32)
     hot = jnp.where(down == iota((pairs, wide), 1), 1.0, 0.0).astype(BF16)
     picks[...] = jnp.concatenate([hot, hot], axis=1)
-    lows = iota((SPREAD * nb, 2 * LANES), 0) // nb
-    for h in range(HIGHS):
-        fold[h] = jnp.where(iota((SPREAD * nb, 2 * LANES), 1) == lows + LOW * h, 1.0, 0.0).astype(BF16)
-
-    same_slot = (iota((HIGHS * nb, SPREAD * nb), 0) & (nb - 1)) == (iota((HIGHS * nb, SPREAD * nb), 1) & (nb - 1))
+    for load in loads[1:]:
+        load.wait()
 
     def weigh(at):
         u = frac_ref[:, at]
@@ -99,9 +109,9 @@
         gw[2, :, at] = g * (-3.0 * cube + 3.0 * square + 3.0 * u + 1.0)
         gw[3, :, at] = g * cube
 
-    def backward(value_ref, first):
+    def backward(value_of, first):
         def block(b, carry):
-            values = value_ref[pl.ds(pl.multiple_of(8 * b, 8), 8), :]
+            values = value_of(b)
             for k in range(8):
                 at = pl.ds(pl.multiple_of((8 * b + k) * LANES, LANES), LANES)
                 if first:
@@ -128,6 +138,8 @@
             return carry
 
         lax.fori_loop(0, tiles // 8, block, 0)
+        if not first:
+            send_norm(image_ref[...], 0)
         grad = jnp.zeros((per_coef, 2 * LANES), F32)
         for h in range(HIGHS):
             chosen = jnp.dot(picks_t[...], jnp.concatenate(split(z[h]), axis=0), preferred_element_type=F32)
@@ -167,33 +179,38 @@
                     )
                     force = force + gw[j, :, at] * found
                 sums.append(jnp.sum(force, axis=0, keepdims=True))
-            im_buf[out, at_coef, pl.ds(pl.multiple_of(8 * b, 8), 8), :] = jnp.concatenate(sums, axis=0)
+            im_buf[out, at_coef, b] = jnp.concatenate(sums, axis=0)
+            each(nc - 1, lambda k: image_copy(out, b, coef_peer(k + 1), at_coef).start())
             return carry
 
         lax.fori_loop(0, tiles // 8, block, 0)
-        im_buf[out, at_coef, tiles:tiles + 8, :] = jnp.broadcast_to(total_of(packed * packed), (8, LANES))
-
-    def copies(kind, phase, step):
-        p = member(step) if kind != "im" else coef_peer(step)
+
+    def image_copy(phase, b, p, slot):
+        return pltpu.make_async_remote_copy(
+            src_ref=im_buf.at[phase, slot, b], dst_ref=im_buf.at[phase, slot, b],
+            send_sem=im_send.at[phase, b, p], recv_sem=im_recv.at[phase, b, slot],
+            device_id=coef_id(p), device_id_type=MESH)
+
+    def image_block(phase, b):
+        def wait(k):
+            p = coef_peer(k + 1)
+            image_copy(phase, b, p, p).wait_recv()
+
+        each(nc - 1, wait)
+        sums = im_buf[phase, 0, b]
+        for p in range(1, nc):
+            sums = sums + im_buf[phase, p, b]
+        return sums
+
+    def copies(kind, phase, step, incoming=False):
+        near = kind == "gm"
+        p = coef_peer(step) if near else member(step)
+        slot = p if incoming else (at_coef if near else me)
+        target = coef_id(p) if near else member_id(p)
         if kind == "rs":
-            count = share + 8 * phase
-            return (send_buf.at[phase, p, pl.ds(0, count)], rs_buf.at[phase, me, pl.ds(0, count)], rs_send.at[phase, p], rs_recv.at[phase, me], member_id(p))
-        if kind == "ag":
-            return (ag_buf.at[phase, me], ag_buf.at[phase, me], ag_send.at[phase, p], ag_recv.at[phase, me], member_id(p))
-        if kind == "im":
-            return (im_buf.at[phase, at_coef], im_buf.at[phase, at_coef], im_send.at[phase, p], im_recv.at[phase, at_coef], coef_id(p))
-        return (fin_buf.at[me], fin_buf.at[me], fin_send.at[p], fin_recv.at[me], member_id(p))
-
-    def landing(kind, phase, step):
-        p = member(step) if kind != "im" else coef_peer(step)
-        if kind == "rs":
-            count = share + 8 * phase
-            return (send_buf.at[phase, p, pl.ds(0, count)], rs_buf.at[phase, p, pl.ds(0, count)], rs_send.at[phase, p], rs_recv.at[phase, p], member_id(p))
-        if kind == "ag":
-            return (ag_buf.at[phase, p], ag_buf.at[phase, p], ag_send.at[phase, p], ag_recv.at[phase, p], member_id(p))
-        if kind == "im":
-            return (im_buf.at[phase, p], im_buf.at[phase, p], im_send.at[phase, p], im_recv.at[phase, p], coef_id(p))
-        return (fin_buf.at[p], fin_buf.at[p], fin_send.at[p], fin_recv.at[p], member_id(p))
+            return (send_buf.at[phase, p], rs_buf.at[phase, slot], rs_send.at[phase, p], rs_recv.at[phase, slot], target)
+        buf, send, recv = dict(ag=(ag_buf, ag_send, ag_recv), gm=(gm_buf, gm_send, gm_recv), nm=(nm_buf, nm_send, nm_recv))[kind]
+        return (buf.at[phase, slot], buf.at[phase, slot], send.at[phase, p], recv.at[phase, slot], target)
 
     def remote(parts):
         return pltpu.make_async_remote_copy(src_ref=parts[0], dst_ref=parts[1], send_sem=parts[2], recv_sem=parts[3], device_id=parts[4], device_id_type=MESH)
@@ -202,16 +219,14 @@
         each(count - 1, lambda k: remote(copies(kind, phase, k + 1)).start())
 
     def arrive(kind, phase, count):
-        each(count - 1, lambda k: remote(landing(kind, phase, k + 1)).wait_recv())
+        each(count - 1, lambda k: remote(copies(kind, phase, k + 1, True)).wait_recv())
 
     def drain(kind, phase, count):
         each(count - 1, lambda k: remote(copies(kind, phase, k + 1)).wait_send())
 
-    def scatter_sum(packed, phase, extra):
+    def scatter_sum(packed, phase):
         for p in range(n):
-            send_buf[phase, p, :share, :] = packed[p * share:(p + 1) * share, :]
-            if extra is not None:
-                send_buf[phase, p, share:share + 8, :] = jnp.broadcast_to(extra, (8, LANES))
+            send_buf[phase, p] = packed[p * share:(p + 1) * share, :]
         start("rs", phase, n)
         rs_buf[phase, me] = send_buf[phase, me]
         arrive("rs", phase, n)
@@ -226,39 +241,49 @@
         arrive("ag", phase, n)
         return ag_buf[phase].reshape(n * share, LANES)
 
-    def exchange(phase):
-        start("im", phase, nc)
-        arrive("im", phase, nc)
-        sums = im_buf[phase, 0]
-        for p in range(1, nc):
-            sums = sums + im_buf[phase, p]
-        return sums[:tiles], sums[tiles:tiles + 1, :1]
-
-    packed = backward(targ_ref, True)
-    send_buf[...] = jnp.zeros(send_buf.shape, F32)
+    def send_gamma(packed, phase):
+        gm_buf[phase, at_coef] = jnp.broadcast_to(total_of(packed * packed), (8, LANES))
+        start("gm", phase, nc)
+
+    def send_norm(image, phase):
+        nm_buf[phase, me] = jnp.broadcast_to(total_of(image * image), (8, LANES))
+        start("nm", phase, n)
+
+    def scalar(kind, buf, phase, count):
+        arrive(kind, phase, count)
+        total = buf[phase, 0, :1, :1]
+        for p in range(1, count):
+            total = total + buf[phase, p, :1, :1]
+        return total
+
+    def target_block(b):
+        return targ_ref[pl.ds(pl.multiple_of(8 * b, 8), 8), :]
+
+    def image_values(b):
+        values = image_block(0, b)
+        image_ref[pl.ds(pl.multiple_of(8 * b, 8), 8), :] = values
+        return values
+
+    packed = backward(target_block, True)
     pl.semaphore_wait(barrier, n - 1 + nc - 1)
-    part = scatter_sum(packed, 0, None)[:share]
+    part = scatter_sum(packed, 0)
     grad = gather(part, 0)
+    send_gamma(grad, 0)
     forward(grad, 0)
-    image, gamma = exchange(0)
-    res_ref[...] = image
-    packed = backward(res_ref, False)
-    sums = scatter_sum(packed, 1, total_of(image * image))
-    alpha = gamma / sums[share:share + 1, :1]
-    part = part - alpha * sums[:share]
-    grad_next = gather(part, 1)
+    packed = backward(image_values, False)
+    sums = scatter_sum(packed, 1)
+    gamma = scalar("gm", gm_buf, 0, nc)
+    alpha = gamma / scalar("nm", nm_buf, 0, n)
+    grad_next = gather(part - alpha * sums, 1)
+    send_gamma(grad_next, 1)
     forward(grad_next, 1)
-    image_next, gamma_next = exchange(1)
+    gamma_next = scalar("gm", gm_buf, 1, nc)
     beta = gamma_next / gamma
-    image_next = image_next + beta * image
-    fin_buf[me] = jnp.broadcast_to(total_of(image_next * image_next), (8, LANES))
-    start("fin", 0, n)
     direction = grad_next + beta * grad
-    arrive("fin", 0, n)
-    norm = fin_buf[0, :1, :1]
-    for p in range(1, n):
-        norm = norm + fin_buf[p, :1, :1]
-    alpha_next = gamma_next / norm
+    image = image_ref[...]
+    image_next = jnp.concatenate([image_block(1, b) for b in range(tiles // 8)], axis=0) + beta * image
+    send_norm(image_next, 1)
+    alpha_next = gamma_next / scalar("nm", nm_buf, 1, n)
     answer = alpha * grad + alpha_next * direction
     sol_ref[:, :LANES] = answer[:per_coef]
     for q, tail in enumerate(tails(answer)):
@@ -267,8 +292,10 @@
     for phase in range(2):
         drain("rs", phase, n)
         drain("ag", phase, n)
-        drain("im", phase, nc)
-    drain("fin", 0, n)
+        drain("gm", phase, nc)
+        drain("nm", phase, n)
+        for b in range(tiles // 8):
+            each(nc - 1, lambda k: image_copy(phase, b, coef_peer(k + 1), at_coef).wait_send())
 
 
 def on_device(n, nd, nc, geometry, fraction, interval, pattern, target):
@@ -283,23 +310,33 @@
     solved, left = pl.pallas_call(
         functools.partial(kernel, n, nd, nc, share),
         out_shape=(jax.ShapeDtypeStruct((per_coef, NK), F32), jax.ShapeDtypeStruct((tiles, LANES), F32)),
-        in_specs=[vmem] * 5,
+        in_specs=[pl.BlockSpec(memory_space=pltpu.MemorySpace.HBM)] * 5,
         out_specs=(vmem, vmem),
         scratch_shapes=[
+            pltpu.VMEM((nb, rows), F32),
+            pltpu.VMEM((nb, rows), F32),
+            pltpu.VMEM((nb, rows), jnp.int32),
+            pltpu.VMEM((nb, tiles), jnp.int32),
+            pltpu.VMEM((tiles, LANES), F32),
+            pltpu.VMEM((tiles, LANES), F32),
             pltpu.VMEM((4, nb, rows), F32),
             pltpu.VMEM((HIGHS, pairs, SPREAD * nb), F32),
             pltpu.VMEM((pairs, 2 * LANES), F32),
             pltpu.VMEM((pairs, 2 * wide), BF16),
             pltpu.VMEM((per_coef, 2 * pairs), BF16),
             pltpu.VMEM((HIGHS, SPREAD * nb, 2 * LANES), BF16),
-            pltpu.VMEM((2, n, share + 8, LANES), F32),
-            pltpu.VMEM((2, n, share + 8, LANES), F32),
             pltpu.VMEM((2, n, share, LANES), F32),
-            pltpu.VMEM((2, nc, tiles + 8, LANES), F32),
-            pltpu.VMEM((n, 8, LANES), F32),
-            sem((2, n)), sem((2, n)), sem((2, n)), sem((2, n)), sem((2, nc)), sem((2, nc)), sem((n,)), sem((n,)),
+            pltpu.VMEM((2, n, share, LANES), F32),
+            pltpu.VMEM((2, n, share, LANES), F32),
+            pltpu.VMEM((2, nc, tiles // 8, 8, LANES), F32),
+            pltpu.VMEM((2, nc, 8, LANES), F32),
+            pltpu.VMEM((2, n, 8, LANES), F32),
+            sem((5,)),
+            sem((2, n)), sem((2, n)), sem((2, n)), sem((2, n)),
+            sem((2, tiles // 8, nc)), sem((2, tiles // 8, nc)),
+            sem((2, nc)), sem((2, nc)), sem((2, n)), sem((2, n)),
         ],
-        compiler_params=pltpu.CompilerParams(collective_id=0, has_side_effects=True, vmem_limit_bytes=40 * 1024 * 1024),
+        compiler_params=pltpu.CompilerParams(collective_id=0, has_side_effects=True, vmem_limit_bytes=63 * 1024 * 1024),
     )(geometry, fraction, interval, pattern, target.reshape(tiles, LANES))
     return solved, left.reshape(rows)
 

time: 45.9 us -> 43.5 us (0.948)
  local copies, waits for them, and re-layouts: 5.45 us -> 2.24 us
  Pallas kernels: 39.5 us -> 40.4 us
    unnamed x12 -> x4, local copies, waits for them, and re-layouts: 5.45 us -> 2.24 us
    pallas_call x1, Pallas kernels: 39.5 us -> 40.4 us  [on_device(): pl.pallas_call(functools.partial(kernel, n, nd, nc, share), out_shape=(ja...]
where the time goes in v2:
time: 43.5 us; the launch traced here: 43.3 us
  Pallas kernels  40.4 us (93%)
  local copies, waits for them, and re-layouts  2.24 us (5%)
  between operations  0.65 us (1%)
    pallas_call x1, Pallas kernels, on_device(): pl.pallas_call(functools.partial(kernel, n, nd, nc, share), out_shape=(ja...  40.4 us
    unnamed x4, local copies, waits for them, and re-layouts  2.24 us

profile of v2, /device:TPU:0, one launch (start us, length us, event | category | flops | bytes accessed | tf_op | source)
XLA Modules:
  0.0 43.3 jit_solution(4409048782551446509)
XLA Ops:
  0.6 40.4 %shard_map.68 = (f32[96,160]{1,0:T(8,128)}, f32[32,128]{1,0:T(8,128)}) custom-call(f32[8,4096]{1,0:T(8,128)} %geom_hbm.1, f32[8,4096]{1,0:T(8,128)} %frac_hbm.1, s32[8,4096]{1,0:T(8,128)} %knot_hbm.1, s32[8,32]{1,0:T(8,128)} %patt_hbm.1, f32[32,128]{1,0:T(8,128)} %bitcast.2), custom_call_target="tpu_custom_call" | custom-call | tf_op jit(solution)/shard_map/pallas_call | solution.py:310
  41.0 0.0 copy-start
  41.1 1.6 %copy.7 = f32[96,160]{0,1:T(8,128)} copy(f32[96,160]{1,0:T(8,128)} %get-tuple-element.6) | data formatting | bytes 122880
  42.7 0.0 copy-done
  42.7 0.6 %copy.9 = f32[4096]{0:T(1024)} copy(f32[4096]{0:T(1024)S(1)} %bitcast.3) | data formatting | bytes 32768
Async XLA Ops:
  41.0 1.6 %copy-start = (f32[32,128]{1,0:T(8,128)S(1)}, f32[32,128]{1,0:T(8,128)}, u32[]{:S(2)}) copy-start(f32[32,128]{1,0:T(8,128)} %get-tuple-element.5) | copy-start | bytes 49156

commit v3 on v2

--- a/solution.py
+++ b/solution.py
@@ -10,9 +10,9 @@
 NK = 160
 TYPES = 384
 LANES = 128
-LOW = 16
-HIGHS = NK // LOW
-SPREAD = LOW + 4
+LOW = 13
+HIGHS = -(-(NK - 3) // LOW)
+SPREAD = LOW + 3
 MESH = pl.DeviceIdType.MESH
 F32 = jnp.float32
 BF16 = jnp.bfloat16
@@ -76,10 +76,13 @@
     each(n - 1, lambda k: pl.semaphore_signal(barrier, inc=1, device_id=member_id(member(k + 1)), device_id_type=MESH))
     each(nc - 1, lambda k: pl.semaphore_signal(barrier, inc=1, device_id=coef_id(coef_peer(k + 1)), device_id_type=MESH))
 
-    lows = iota((SPREAD * nb, 2 * LANES), 0) // nb
+    inner = SPREAD * nb
+    lows = iota((inner, 2 * LANES), 0) // nb
     for h in range(HIGHS):
-        fold[h] = jnp.where(iota((SPREAD * nb, 2 * LANES), 1) == lows + LOW * h, 1.0, 0.0).astype(BF16)
-    same_slot = (iota((HIGHS * nb, SPREAD * nb), 0) & (nb - 1)) == (iota((HIGHS * nb, SPREAD * nb), 1) & (nb - 1))
+        hot = jnp.where(iota((inner, 2 * LANES), 1) == lows + LOW * h, 1.0, 0.0).astype(BF16)
+        fold[2 * h * inner:(2 * h + 1) * inner, :] = hot
+        fold[(2 * h + 1) * inner:(2 * h + 2) * inner, :] = hot
+    same_slot = (iota((nb, inner), 1) & (nb - 1)) == iota((nb, inner), 0)
 
     loads[0].wait()
     kinds = patt_ref[...].astype(F32).astype(BF16)
@@ -112,12 +115,13 @@
     def backward(value_of, first):
         def block(b, carry):
             values = value_of(b)
-            for k in range(8):
+            def product(k):
                 at = pl.ds(pl.multiple_of((8 * b + k) * LANES, LANES), LANES)
                 if first:
                     weigh(at)
                 knot = knot_ref[:, at]
-                high, low = knot >> 4, knot & (LOW - 1)
+                high = (knot * 79) >> 10
+                low = knot - LOW * high
                 value = values[k:k + 1, :]
                 terms = [gw[j, :, at] * value for j in range(4)]
                 hits = [low == m for m in range(LOW)]
@@ -129,22 +133,25 @@
                             part = jnp.where(hits[m - j], terms[j], part)
                     parts.append(part)
                 right = jnp.concatenate(split(jnp.concatenate(parts, axis=0)), axis=1)
-                left = jnp.concatenate([jnp.where(high == h, 1.0, 0.0) for h in range(HIGHS)], axis=0).astype(BF16)
+                left = [jnp.where(high == h, 1.0, 0.0) for h in range(HIGHS)]
+                left = jnp.concatenate(left + [jnp.zeros((nb, LANES), F32)] * (HIGHS % 2), axis=0).astype(BF16)
                 left = jnp.concatenate([left, left], axis=1)
                 prod = lax.dot_general(left, right, (((1,), (1,)), ((), ())), preferred_element_type=F32)
-                prod = jnp.where(same_slot, prod, 0.0)
-                for h in range(HIGHS):
-                    z[h, pl.ds(pl.multiple_of((8 * b + k) * nb, nb), nb), :] = prod[h * nb:(h + 1) * nb, :]
+                return [jnp.where(same_slot, prod[h * nb:(h + 1) * nb, :], 0.0) for h in range(HIGHS)]
+
+            for k in range(0, 8, 2):
+                span = pl.ds(pl.multiple_of((8 * b + k) * nb, 2 * nb), 2 * nb)
+                for h, two in enumerate(zip(product(k), product(k + 1))):
+                    top, rest = split(jnp.concatenate(two, axis=0))
+                    z[span, 2 * h * inner:(2 * h + 1) * inner] = top
+                    z[span, (2 * h + 1) * inner:(2 * h + 2) * inner] = rest
             return carry
 
         lax.fori_loop(0, tiles // 8, block, 0)
         if not first:
             send_norm(image_ref[...], 0)
-        grad = jnp.zeros((per_coef, 2 * LANES), F32)
-        for h in range(HIGHS):
-            chosen = jnp.dot(picks_t[...], jnp.concatenate(split(z[h]), axis=0), preferred_element_type=F32)
-            for piece in split(chosen):
-                grad = grad + jnp.dot(piece, fold[h], preferred_element_type=F32)
+        folded = jnp.dot(z[...], fold[...], preferred_element_type=F32)
+        grad = jnp.dot(picks_t[...], jnp.concatenate(split(folded), axis=0), preferred_element_type=F32)
         tail = grad[:quarter, LANES:]
         for q in range(1, 4):
             tail = tail + pltpu.roll(grad[q * quarter:(q + 1) * quarter, LANES:], 32 * q, 1)
@@ -285,9 +292,9 @@
     send_norm(image_next, 1)
     alpha_next = gamma_next / scalar("nm", nm_buf, 1, n)
     answer = alpha * grad + alpha_next * direction
-    sol_ref[:, :LANES] = answer[:per_coef]
-    for q, tail in enumerate(tails(answer)):
-        sol_ref[q * quarter:(q + 1) * quarter, LANES:] = tail[:, :NK - LANES]
+    tail = jnp.concatenate(tails(answer), axis=0)
+    sol_ref[:LANES, :] = answer[:per_coef].T
+    sol_ref[LANES:, :] = tail.T[:NK - LANES, :]
     res_ref[...] = targ_ref[...] - alpha * image - alpha_next * image_next
     for phase in range(2):
         drain("rs", phase, n)
@@ -309,7 +316,7 @@
     vmem = pl.BlockSpec(memory_space=pltpu.VMEM)
     solved, left = pl.pallas_call(
         functools.partial(kernel, n, nd, nc, share),
-        out_shape=(jax.ShapeDtypeStruct((per_coef, NK), F32), jax.ShapeDtypeStruct((tiles, LANES), F32)),
+        out_shape=(jax.ShapeDtypeStruct((NK, per_coef), F32), jax.ShapeDtypeStruct((tiles, LANES), F32)),
         in_specs=[pl.BlockSpec(memory_space=pltpu.MemorySpace.HBM)] * 5,
         out_specs=(vmem, vmem),
         scratch_shapes=[
@@ -320,11 +327,11 @@
             pltpu.VMEM((tiles, LANES), F32),
             pltpu.VMEM((tiles, LANES), F32),
             pltpu.VMEM((4, nb, rows), F32),
-            pltpu.VMEM((HIGHS, pairs, SPREAD * nb), F32),
+            pltpu.VMEM((pairs, 2 * HIGHS * SPREAD * nb), BF16),
             pltpu.VMEM((pairs, 2 * LANES), F32),
             pltpu.VMEM((pairs, 2 * wide), BF16),
             pltpu.VMEM((per_coef, 2 * pairs), BF16),
-            pltpu.VMEM((HIGHS, SPREAD * nb, 2 * LANES), BF16),
+            pltpu.VMEM((2 * HIGHS * SPREAD * nb, 2 * LANES), BF16),
             pltpu.VMEM((2, n, share, LANES), F32),
             pltpu.VMEM((2, n, share, LANES), F32),
             pltpu.VMEM((2, n, share, LANES), F32),
@@ -338,7 +345,7 @@
         ],
         compiler_params=pltpu.CompilerParams(collective_id=0, has_side_effects=True, vmem_limit_bytes=63 * 1024 * 1024),
     )(geometry, fraction, interval, pattern, target.reshape(tiles, LANES))
-    return solved, left.reshape(rows)
+    return solved.T, left.reshape(rows)
 
 
 def solution(mesh):

time: 43.5 us -> 42.9 us (0.986)
  Pallas kernels: 40.4 us -> 39.9 us
    pallas_call x1, Pallas kernels: 40.4 us -> 39.9 us  [on_device(): pl.pallas_call(functools.partial(kernel, n, nd, nc, share), out_shape=(ja...]
where the time goes in v3:
time: 42.9 us; the launch traced here: 42.7 us
  Pallas kernels  39.9 us (93%)
  local copies, waits for them, and re-layouts  2.14 us (5%)
  between operations  0.65 us (2%)
    pallas_call x1, Pallas kernels, on_device(): pl.pallas_call(functools.partial(kernel, n, nd, nc, share), out_shape=(ja...  39.9 us
    unnamed x4, local copies, waits for them, and re-layouts  2.14 us

profile of v3, /device:TPU:0, one launch (start us, length us, event | category | flops | bytes accessed | tf_op | source)
XLA Modules:
  0.0 42.7 jit_solution(17028154793929196819)
XLA Ops:
  0.6 39.9 %shard_map.68 = (f32[160,96]{1,0:T(8,128)}, f32[32,128]{1,0:T(8,128)}) custom-call(f32[8,4096]{1,0:T(8,128)} %geom_hbm.1, f32[8,4096]{1,0:T(8,128)} %frac_hbm.1, s32[8,4096]{1,0:T(8,128)} %knot_hbm.1, s32[8,32]{1,0:T(8,128)} %patt_hbm.1, f32[32,128]{1,0:T(8,128)} %bitcast.4), custom_call_target="tpu_custom_call" | custom-call | tf_op jit(solution)/shard_map/pallas_call | solution.py:317
  40.5 0.0 copy-start
  40.5 1.5 %copy.9 = f32[96,160]{0,1:T(8,128)} copy(f32[96,160]{0,1:T(8,128)} %bitcast.3) | data formatting | bytes 122880
  42.1 0.0 copy-done
  42.1 0.6 %copy.10 = f32[4096]{0:T(1024)} copy(f32[4096]{0:T(1024)S(1)} %bitcast.5) | data formatting | bytes 32768
Async XLA Ops:
  40.5 1.5 %copy-start = (f32[32,128]{1,0:T(8,128)S(1)}, f32[32,128]{1,0:T(8,128)}, u32[]{:S(2)}) copy-start(f32[32,128]{1,0:T(8,128)} %get-tuple-element.5) | copy-start | bytes 49156

commit v4 on v3

--- a/solution.py
+++ b/solution.py
@@ -39,10 +39,10 @@
         lax.fori_loop(0, count, lambda index, _: (body(index), 0)[1], 0)
 
 
-def kernel(n, nd, nc, share, geom_hbm, frac_hbm, knot_hbm, patt_hbm, targ_hbm, sol_ref, res_ref,
+def kernel(nf, nd, nc, share, geom_hbm, frac_hbm, knot_hbm, patt_hbm, targ_hbm, sol_ref, res_ref,
            geom_ref, frac_ref, knot_ref, patt_ref, targ_ref, image_ref,
-           gw, z, table, picks, picks_t, fold, send_buf, rs_buf, ag_buf, im_buf, gm_buf, nm_buf, load_sem,
-           rs_send, rs_recv, ag_send, ag_recv, im_send, im_recv, gm_send, gm_recv, nm_send, nm_recv):
+           gw, z, table, picks, picks_t, fold, send_buf, rs_buf, fr_buf, ag_buf, im_buf, gm_buf, nm_buf, load_sem,
+           rs_send, rs_recv, fr_send, fr_recv, ag_send, ag_recv, im_send, im_recv, gm_send, gm_recv, nm_send, nm_recv):
     loads = [
         pltpu.make_async_copy(src, dst, load_sem.at[k])
         for k, (src, dst) in enumerate(((patt_hbm, patt_ref), (frac_hbm, frac_ref), (geom_hbm, geom_ref), (knot_hbm, knot_ref), (targ_hbm, targ_ref)))
@@ -59,6 +59,7 @@
     at_coef = lax.axis_index("coef")
     at_frame = lax.axis_index("frame")
     me = at_frame * nd + at_dom
+    n = nf * nd
 
     def member(step):
         return lax.rem(me + step, n)
@@ -71,6 +72,12 @@
 
     def coef_id(p):
         return (at_frame, at_dom, p)
+
+    def dom_peer(step):
+        return lax.rem(at_dom + step, nd)
+
+    def frame_peer(step):
+        return lax.rem(at_frame + step, nf)
 
     barrier = pltpu.get_barrier_semaphore()
     each(n - 1, lambda k: pl.semaphore_signal(barrier, inc=1, device_id=member_id(member(k + 1)), device_id_type=MESH))
@@ -156,7 +163,7 @@
         for q in range(1, 4):
             tail = tail + pltpu.roll(grad[q * quarter:(q + 1) * quarter, LANES:], 32 * q, 1)
         filled = per_coef + quarter
-        return jnp.concatenate([grad[:, :LANES], tail, jnp.zeros((n * share - filled, LANES), F32)], axis=0)
+        return jnp.concatenate([grad[:, :LANES], tail, jnp.zeros((nd * share - filled, LANES), F32)], axis=0)
 
     def tails(packed):
         tail = packed[per_coef:per_coef + quarter, :]
@@ -210,14 +217,20 @@
         return sums
 
     def copies(kind, phase, step, incoming=False):
-        near = kind == "gm"
-        p = coef_peer(step) if near else member(step)
-        slot = p if incoming else (at_coef if near else me)
-        target = coef_id(p) if near else member_id(p)
+        p, mine, target = {
+            "rs": lambda: (dom_peer(step), at_dom, lambda q: (at_frame, q, at_coef)),
+            "fr": lambda: (frame_peer(step), at_frame, lambda q: (q, at_dom, at_coef)),
+            "ag": lambda: (dom_peer(step), at_dom, lambda q: (at_frame, q, at_coef)),
+            "gm": lambda: (coef_peer(step), at_coef, coef_id),
+            "nm": lambda: (member(step), me, member_id),
+        }[kind]()
+        slot = p if incoming else mine
         if kind == "rs":
-            return (send_buf.at[phase, p], rs_buf.at[phase, slot], rs_send.at[phase, p], rs_recv.at[phase, slot], target)
-        buf, send, recv = dict(ag=(ag_buf, ag_send, ag_recv), gm=(gm_buf, gm_send, gm_recv), nm=(nm_buf, nm_send, nm_recv))[kind]
-        return (buf.at[phase, slot], buf.at[phase, slot], send.at[phase, p], recv.at[phase, slot], target)
+            return (send_buf.at[phase, p], rs_buf.at[phase, slot], rs_send.at[phase, p], rs_recv.at[phase, slot], target(p))
+        buf, send, recv = dict(
+            fr=(fr_buf, fr_send, fr_recv), ag=(ag_buf, ag_send, ag_recv),
+            gm=(gm_buf, gm_send, gm_recv), nm=(nm_buf, nm_send, nm_recv))[kind]
+        return (buf.at[phase, slot], buf.at[phase, slot], send.at[phase, p], recv.at[phase, slot], target(p))
 
     def remote(parts):
         return pltpu.make_async_remote_copy(src_ref=parts[0], dst_ref=parts[1], send_sem=parts[2], recv_sem=parts[3], device_id=parts[4], device_id_type=MESH)
@@ -232,21 +245,27 @@
         each(count - 1, lambda k: remote(copies(kind, phase, k + 1)).wait_send())
 
     def scatter_sum(packed, phase):
-        for p in range(n):
+        for p in range(nd):
             send_buf[phase, p] = packed[p * share:(p + 1) * share, :]
-        start("rs", phase, n)
-        rs_buf[phase, me] = send_buf[phase, me]
-        arrive("rs", phase, n)
+        start("rs", phase, nd)
+        rs_buf[phase, at_dom] = send_buf[phase, at_dom]
+        arrive("rs", phase, nd)
         sums = rs_buf[phase, 0]
-        for p in range(1, n):
+        for p in range(1, nd):
             sums = sums + rs_buf[phase, p]
+        fr_buf[phase, at_frame] = sums
+        start("fr", phase, nf)
+        arrive("fr", phase, nf)
+        sums = fr_buf[phase, 0]
+        for p in range(1, nf):
+            sums = sums + fr_buf[phase, p]
         return sums
 
     def gather(part, phase):
-        ag_buf[phase, me] = part
-        start("ag", phase, n)
-        arrive("ag", phase, n)
-        return ag_buf[phase].reshape(n * share, LANES)
+        ag_buf[phase, at_dom] = part
+        start("ag", phase, nd)
+        arrive("ag", phase, nd)
+        return ag_buf[phase].reshape(nd * share, LANES)
 
     def send_gamma(packed, phase):
         gm_buf[phase, at_coef] = jnp.broadcast_to(total_of(packed * packed), (8, LANES))
@@ -297,25 +316,27 @@
     sol_ref[LANES:, :] = tail.T[:NK - LANES, :]
     res_ref[...] = targ_ref[...] - alpha * image - alpha_next * image_next
     for phase in range(2):
-        drain("rs", phase, n)
-        drain("ag", phase, n)
+        drain("rs", phase, nd)
+        drain("fr", phase, nf)
+        drain("ag", phase, nd)
         drain("gm", phase, nc)
         drain("nm", phase, n)
         for b in range(tiles // 8):
             each(nc - 1, lambda k: image_copy(phase, b, coef_peer(k + 1), at_coef).wait_send())
 
 
-def on_device(n, nd, nc, geometry, fraction, interval, pattern, target):
+def on_device(nf, nd, nc, geometry, fraction, interval, pattern, target):
     nb, rows = geometry.shape
     tiles = rows // LANES
     pairs = tiles * nb
     per_coef = TYPES // nc
     wide = -(-per_coef // LANES) * LANES
-    share = -(-(per_coef + per_coef // 4) // (8 * n)) * 8
+    n = nf * nd
+    share = -(-(per_coef + per_coef // 4) // (8 * nd)) * 8
     sem = pltpu.SemaphoreType.DMA
     vmem = pl.BlockSpec(memory_space=pltpu.VMEM)
     solved, left = pl.pallas_call(
-        functools.partial(kernel, n, nd, nc, share),
+        functools.partial(kernel, nf, nd, nc, share),
         out_shape=(jax.ShapeDtypeStruct((NK, per_coef), F32), jax.ShapeDtypeStruct((tiles, LANES), F32)),
         in_specs=[pl.BlockSpec(memory_space=pltpu.MemorySpace.HBM)] * 5,
         out_specs=(vmem, vmem),
@@ -332,14 +353,15 @@
             pltpu.VMEM((pairs, 2 * wide), BF16),
             pltpu.VMEM((per_coef, 2 * pairs), BF16),
             pltpu.VMEM((2 * HIGHS * SPREAD * nb, 2 * LANES), BF16),
-            pltpu.VMEM((2, n, share, LANES), F32),
-            pltpu.VMEM((2, n, share, LANES), F32),
-            pltpu.VMEM((2, n, share, LANES), F32),
+            pltpu.VMEM((2, nd, share, LANES), F32),
+            pltpu.VMEM((2, nd, share, LANES), F32),
+            pltpu.VMEM((2, nf, share, LANES), F32),
+            pltpu.VMEM((2, nd, share, LANES), F32),
             pltpu.VMEM((2, nc, tiles // 8, 8, LANES), F32),
             pltpu.VMEM((2, nc, 8, LANES), F32),
             pltpu.VMEM((2, n, 8, LANES), F32),
             sem((5,)),
-            sem((2, n)), sem((2, n)), sem((2, n)), sem((2, n)),
+            sem((2, nd)), sem((2, nd)), sem((2, nf)), sem((2, nf)), sem((2, nd)), sem((2, nd)),
             sem((2, tiles // 8, nc)), sem((2, tiles // 8, nc)),
             sem((2, nc)), sem((2, nc)), sem((2, n)), sem((2, n)),
         ],
@@ -350,10 +372,10 @@
 
 def solution(mesh):
     sizes = dict(mesh.shape)
-    n, nd, nc = sizes["frame"] * sizes["dom"], sizes["dom"], sizes["coef"]
+    nf, nd, nc = sizes["frame"], sizes["dom"], sizes["coef"]
     both = P("coef", ("frame", "dom"))
     return jax.shard_map(
-        functools.partial(on_device, n, nd, nc),
+        functools.partial(on_device, nf, nd, nc),
         mesh=mesh,
         in_specs=(both, both, both, both, P(("frame", "dom"))),
         out_specs=(P("coef", None), P(("frame", "dom"))),

time: 42.9 us -> 46 us (1.072)
  Pallas kernels: 39.9 us -> 43 us
    pallas_call x1, Pallas kernels: 39.9 us -> 43 us  [on_device(): pl.pallas_call(functools.partial(kernel, nf, nd, nc, share), out_shape=(j...]
where the time goes in v4:
time: 46 us; the launch traced here: 45.8 us
  Pallas kernels  43 us (93%)
  local copies, waits for them, and re-layouts  2.14 us (5%)
  between operations  0.65 us (1%)
    pallas_call x1, Pallas kernels, on_device(): pl.pallas_call(functools.partial(kernel, nf, nd, nc, share), out_shape=(j...  43 us
    unnamed x4, local copies, waits for them, and re-layouts  2.14 us

profile of v4, /device:TPU:0, one launch (start us, length us, event | category | flops | bytes accessed | tf_op | source)
XLA Modules:
  0.0 45.8 jit_solution(8687486412273410523)
XLA Ops:
  0.6 43.0 %shard_map.68 = (f32[160,96]{1,0:T(8,128)}, f32[32,128]{1,0:T(8,128)}) custom-call(f32[8,4096]{1,0:T(8,128)} %geom_hbm.1, f32[8,4096]{1,0:T(8,128)} %frac_hbm.1, s32[8,4096]{1,0:T(8,128)} %knot_hbm.1, s32[8,32]{1,0:T(8,128)} %patt_hbm.1, f32[32,128]{1,0:T(8,128)} %bitcast.4), custom_call_target="tpu_custom_call" | custom-call | tf_op jit(solution)/shard_map/pallas_call | solution.py:338
  43.6 0.0 copy-start
  43.6 1.5 %copy.9 = f32[96,160]{0,1:T(8,128)} copy(f32[96,160]{0,1:T(8,128)} %bitcast.3) | data formatting | bytes 122880
  45.2 0.0 copy-done
  45.2 0.6 %copy.10 = f32[4096]{0:T(1024)} copy(f32[4096]{0:T(1024)S(1)} %bitcast.5) | data formatting | bytes 32768
Async XLA Ops:
  43.6 1.5 %copy-start = (f32[32,128]{1,0:T(8,128)S(1)}, f32[32,128]{1,0:T(8,128)}, u32[]{:S(2)}) copy-start(f32[32,128]{1,0:T(8,128)} %get-tuple-element.5) | copy-start | bytes 49156
